TPU v7x, 256 devices: a whole 4x4x8 slice. The times are simulated.
256 devices in a mesh: seq: 32 (over z, x_hi, core), head: 8 (over x_lo, y).
Axes of the slice: x: 4 (x_hi: 2, x_lo: 2; x = x_hi * 2 + x_lo), y: 4, z: 8, core: 2. Of those that a mesh axis runs over, the one named last changes fastest.
Arguments:
- queries: bfloat16 [128, 2, 8192], P('seq', None, 'head'), may hold values from -7 to 7
- prefix_keys: bfloat16 [131072, 8, 128], P('seq', 'head'), may hold values from -15 to 15
- prefix_values: bfloat16 [131072, 8, 128], P('seq', 'head'), may hold values from -12 to 12
- suffix_keys: bfloat16 [128, 4096, 8, 128], P('seq', None, 'head'), may hold values from -19 to 19
- suffix_values: bfloat16 [128, 4096, 8, 128], P('seq', None, 'head'), may hold values from -12 to 12
- new_keys: bfloat16 [128, 2, 8, 128], P('seq', None, 'head'), may hold values from -8 to 8
- new_values: bfloat16 [128, 2, 8, 128], P('seq', None, 'head'), may hold values from -12 to 12
- suffix_lengths: int32 [128], P('seq'), may hold values from 1 to 4096, 262144 in all
- out_weight: bfloat16 [8192, 8192], P('head', 'seq'), may hold values from -0.0625 to 0.0625
Outputs:
- layer_output: bfloat16 [128, 2, 8192], P('head', None, 'seq')
Inputs may be any that keep to these rules, and one draw needn't show every extreme that they name: `suffix_lengths`: the longest suffix holds exactly 4096 tokens.
All inputs are finite; a program needn't handle non-finite values. No bound on the sum of `suffix_lengths` on one device may be relied on, other than what follows from the above.
Results may differ from a plain program's by a relative error of at most 0.015.
Values may be sent and summed in bfloat16 or wider, within the bound.
No kernel may reach another device: no remote copies, remote signals or barrier semaphores. Data moves between devices by JAX's collectives and lax.ppermute only.
A program may use at most 192 MiB of HBM per device.

v0:
```python
import jax
import jax.numpy as jnp
from jax import lax
from jax.sharding import PartitionSpec as P

masked_score = -1e30


def combine_parts(left_part, right_part):
    maximum = jnp.maximum(left_part[0], right_part[0])
    left_scale = jnp.exp(left_part[0] - maximum)
    right_scale = jnp.exp(right_part[0] - maximum)
    totals = left_part[1] * left_scale + right_part[1] * right_scale
    numerator = left_part[2] * left_scale[..., None] + right_part[2] * right_scale[..., None]
    return (maximum, totals, numerator)


def prefix_partial(query_rows, key_rows, value_rows, score_scale):
    positions, head_dim = key_rows.shape
    block_len = min(1024, positions)
    key_blocks = key_rows.reshape(positions // block_len, block_len, head_dim)
    value_blocks = value_rows.reshape(positions // block_len, block_len, head_dim)

    def advance(running, blocks):
        maximum, totals, numerator = running
        key_block, value_block = blocks
        scores = (
            jnp.einsum("nd,kd->nk", query_rows, key_block, preferred_element_type=jnp.float32)
            * score_scale
        )
        new_max = jnp.maximum(maximum, jnp.max(scores, axis=1))
        rescale = jnp.exp(maximum - new_max)
        weights = jnp.exp(scores - new_max[:, None])
        totals = totals * rescale + jnp.sum(weights, axis=1)
        numerator = numerator * rescale[:, None] + jnp.dot(
            weights.astype(jnp.bfloat16), value_block, preferred_element_type=jnp.float32
        )
        return ((new_max, totals, numerator), None)

    count_rows = query_rows.shape[0]
    initial = (
        jnp.full((count_rows,), masked_score, jnp.float32),
        jnp.zeros((count_rows,), jnp.float32),
        jnp.zeros((count_rows, head_dim), jnp.float32),
    )
    result, unused = lax.scan(advance, initial, (key_blocks, value_blocks))
    return result


def fresh_state(query_rows, key_rows, value_rows, score_scale):
    scores = (
        jnp.einsum("rtjd,rud->rtju", query_rows, key_rows, preferred_element_type=jnp.float32)
        * score_scale
    )
    step_count = scores.shape[1]
    causal = (jnp.arange(step_count)[:, None] >= jnp.arange(step_count)[None, :])[None, :, None, :]
    maximum = jnp.max(jnp.where(causal, scores, masked_score), axis=-1)
    weights = jnp.where(causal, jnp.exp(scores - maximum[..., None]), 0.0)
    numerator = jnp.einsum(
        "rtju,rud->rtjd",
        weights.astype(jnp.bfloat16),
        value_rows,
        preferred_element_type=jnp.float32,
    )
    return (maximum, jnp.sum(weights, axis=-1), numerator)


def suffix_block(partial_value, query_rows, key_block, value_block, allowed, score_scale):
    maximum, totals, numerator = partial_value
    scores = (
        jnp.einsum("rtjd,rsd->rtjs", query_rows, key_block, preferred_element_type=jnp.float32)
        * score_scale
    )
    new_max = jnp.maximum(maximum, jnp.max(jnp.where(allowed, scores, masked_score), axis=-1))
    rescale = jnp.exp(maximum - new_max)
    weights = jnp.where(allowed, jnp.exp(scores - new_max[..., None]), 0.0)
    totals = totals * rescale + jnp.sum(weights, axis=-1)
    numerator = numerator * rescale[..., None] + jnp.einsum(
        "rtjs,rsd->rtjd",
        weights.astype(jnp.bfloat16),
        value_block,
        preferred_element_type=jnp.float32,
    )
    return (new_max, totals, numerator)


def suffix_padded(partial_value, query_rows, key_rows, value_rows, lengths, score_scale):
    slots = key_rows.shape[1]
    allowed = (jnp.arange(slots)[None, :] < lengths[:, None])[:, None, None, :]
    return suffix_block(partial_value, query_rows, key_rows, value_rows, allowed, score_scale)


def shards(
    queries,
    prefix_keys,
    prefix_values,
    suffix_keys,
    suffix_values,
    new_keys,
    new_values,
    suffix_lengths,
    out_weight,
):
    owned, step_count, row_width = queries.shape
    local_heads = prefix_keys.shape[1]
    head_dim = prefix_keys.shape[2]
    group_size = row_width // (local_heads * head_dim)
    score_scale = head_dim ** (-0.5)
    everyone = owned * lax.axis_size("seq")

    def absorb(portion):
        span_rows = portion.shape[0]
        by_head = portion.reshape(span_rows, step_count, local_heads, group_size, head_dim)
        flat_rows = by_head[:, :, 0].reshape(span_rows * step_count * group_size, head_dim)
        outcomes = [
            prefix_partial(flat_rows, prefix_keys[:, 0, :], prefix_values[:, 0, :], score_scale)
        ]
        maximum = jnp.stack(
            [outcome[0].reshape(span_rows, step_count, group_size) for outcome in outcomes], axis=2
        )
        totals = jnp.stack(
            [outcome[1].reshape(span_rows, step_count, group_size) for outcome in outcomes], axis=2
        )
        numerator = jnp.stack(
            [
                outcome[2].reshape(span_rows, step_count, group_size, head_dim)
                for outcome in outcomes
            ],
            axis=2,
        )
        return tuple((update for update in (maximum, totals, numerator)))

    gathered = absorb(lax.all_gather(queries, "seq", axis=0, tiled=True))
    own_queries = queries.reshape(owned, step_count, local_heads, group_size, head_dim)
    query_rows = own_queries[:, :, 0]
    partial_value = fresh_state(
        query_rows, new_keys[:, :, 0, :], new_values[:, :, 0, :], score_scale
    )
    partial_value = suffix_padded(
        partial_value,
        query_rows,
        suffix_keys[:, :, 0, :],
        suffix_values[:, :, 0, :],
        suffix_lengths,
        score_scale,
    )
    own_parts = [partial_value]
    own_state = tuple(
        (jnp.stack([outcome[member] for outcome in own_parts], axis=2) for member in range(3))
    )
    start_row = lax.axis_index("seq") * owned
    owned_part = tuple(
        (lax.dynamic_slice_in_dim(stored, start_row, owned, 0) for stored in gathered)
    )
    joined = combine_parts(owned_part, own_state)
    maximum, totals, numerator = tuple(
        (
            lax.dynamic_update_slice_in_dim(stored, update, start_row, 0)
            for stored, update in zip(gathered, joined)
        )
    )
    global_max = lax.pmax(maximum, "seq")
    rescale = jnp.exp(maximum - global_max)
    all_numerator, all_totals = lax.psum((numerator * rescale[..., None], totals * rescale), "seq")
    attended = (
        (all_numerator / all_totals[..., None])
        .astype(jnp.bfloat16)
        .reshape(everyone, step_count, row_width)
    )
    summed = lax.psum_scatter(
        jnp.einsum("rtk,kc->rtc", attended, out_weight, preferred_element_type=jnp.float32),
        "head",
        scatter_dimension=0,
        tiled=True,
    )
    return summed.astype(jnp.bfloat16)


def solution(mesh):
    placed = (
        P("seq", None, "head"),
        P("seq", "head", None),
        P("seq", "head", None),
        P("seq", None, "head", None),
        P("seq", None, "head", None),
        P("seq", None, "head", None),
        P("seq", None, "head", None),
        P("seq"),
        P("head", "seq"),
    )
    return jax.shard_map(
        shards, mesh=mesh, in_specs=placed, out_specs=P("head", None, "seq"), check_vma=False
    )
```

profile of v0, /device:TPU:1, one launch (start us, length us, event | category | flops | bytes accessed | tf_op | source)
XLA Modules:
  0.0 560.7 jit_solution(7011451756623933386)
XLA Ops:
  6.6 47.9 %all_gather.3 = bf16[128,2,1024]{2,1,0:T(2,128)(2,1)S(1)} all-gather(bf16[4,2,1024]{2,1,0:T(2,128)(2,1)} %param.11), channel_id=1, replica_groups=mesh['seq'=32,'head'=8] {'seq'}, dimensions={0}, use_global_device_ids=true | all-gather | bytes 540672 | tf_op jit(solution)/shard_map/all_gather | solution.py:133
  54.4 0.7 squeeze_reshape.3
  55.2 0.3 reshape_squeeze_reshape.3
  55.5 56.6 %while.15 = (s32[]{:T(128)}, f32[2048]{0:T(1024)S(1)}, f32[2048]{0:T(1024)S(1)}, f32[2048,128]{1,0:T(8,128)S(1)}, bf16[4,1024,128]{2,1,0:T(8,128)(2,1)}, /*index...) while((s32[]{:T(128)}, f32[2048]{0:T(1024)S(1)}, ...), condition=%wide.region_3.4_spmd.clone, body=%wide.region_0.3_spmd.clone.sunk | while | flops 1091315712 | bytes 61997204 | solution.py:46
  55.5 5.4 multiply_reduce_fusion.2
  61.0 4.9 fusion.70
  65.9 0.8 copy-done.1
  66.7 2.9 fusion.72
  69.7 5.4 multiply_reduce_fusion.2
  75.1 4.9 fusion.70
  80.1 0.8 copy-done.1
  80.9 2.9 fusion.72
  83.8 5.4 multiply_reduce_fusion.2
  89.3 4.9 fusion.70
  94.2 0.8 copy-done.1
  95.0 2.9 fusion.72
  98.0 5.4 multiply_reduce_fusion.2
  103.4 4.9 fusion.70
  108.4 0.8 copy-done.1
  109.2 2.9 fusion.72
  113.0 3.5 select_reduce_fusion
  116.5 0.4 fusion.36
  116.9 123.1 %pmax.7 = f32[128,2,1,8]{3,1,0,2:T(2,128)S(1)} all-reduce(f32[128,2,1,8]{3,1,0,2:T(2,128)S(1)} %get-tuple-element.95), channel_id=1, replica_groups=mesh['seq'=32,'head'=8] {'seq'}, use_global_device_ids=true, to_apply=%region_6.7 | all-reduce | flops 2048 | bytes 16384 | tf_op jit(solution)/shard_map/pmax | solution.py:162
  240.4 2.9 fusion.33
  243.4 1.4 broadcast_multiply_fusion
  244.8 128.6 %psum.15 = f32[128,2,8]{2,1,0:T(2,128)S(1)} all-reduce(f32[128,2,8]{2,1,0:T(2,128)S(1)} %get-tuple-element.91), channel_id=1, replica_groups=mesh['seq'=32,'head'=8] {'seq'}, use_global_device_ids=true, to_apply=%region_10.11 | all-reduce | flops 2048 | bytes 16384 | tf_op jit(solution)/shard_map/psum | solution.py:164
  373.4 143.1 %all-reduce.2.cloned.1.call-done = f32[128,2,1,8,128]{4,3,1,0,2:T(8,128)} async-done(((f32[128,2,1,8,128]{4,3,1,0,2:T(8,128)}), f32[128,2,1,8,128]{4,3,1,0,2:T(8,128)}) %all-reduce.2.cloned.1.call-update) | async-done | bytes 1048592 | tf_op jit(solution)/shard_map/psum | solution.py:164
  516.5 1.6 divide_convert_fusion
  518.3 1.0 fusion.39
  519.3 33.1 %reduce-scatter.2.cloned.1.call-done = f32[16,2,256]{2,0,1:T(8,128)} async-done(((f32[128,2,256]{2,0,1:T(8,128)}), f32[16,2,256]{2,0,1:T(8,128)}) %reduce-scatter.2.cloned.1.call-update) | async-done | bytes 32784 | tf_op jit(solution)/shard_map/reduce_scatter | solution.py:170
  552.4 0.8 convert_element_type.19
  553.2 0.6 copy.15
  (42 shorter events, 1.6 us)
Async XLA Ops:
  6.5 511.7 %copy-start = (bf16[1024,256]{1,0:T(8,128)(2,1)S(1)}, bf16[1024,256]{1,0:T(8,128)(2,1)}, u32[]{:S(2)}) copy-start(bf16[1024,256]{1,0:T(8,128)(2,1)} %param.19) | copy-start | bytes 1572868
  6.5 510.0 %all-reduce.2.cloned.1.call-start = ((), (), s32[]{:S(2)}) async-start(), calls=%async_computation.1 | async-start | bytes 2097152 | tf_op jit(solution)/shard_map/psum | solution.py:164
  55.5 56.7 %copy-start.2 = (s32[4]{0:T(128)S(1)}, s32[4]{0:T(128)}, u32[]{:S(2)}) copy-start(s32[4]{0:T(128)} %param.18) | copy-start | bytes 52
  55.5 57.2 %copy-start.3 = (bf16[4,2,1,128]{3,1,2,0:T(2,128)(2,1)S(1)}, bf16[4,2,1,128]{3,1,2,0:T(2,128)(2,1)}, u32[]{:S(2)}) copy-start(bf16[4,2,1,128]{3,1,2,0:T(2,128)(2,1)} %param.16) | copy-start | bytes 6148
  61.0 5.8 %copy-start.1 = (f32[1024,2048]{1,0:T(8,128)S(1)}, f32[1024,2048]{1,0:T(8,128)}, u32[]{:S(2)}) copy-start(f32[1024,2048]{1,0:T(8,128)} %get-tuple-element.151) | copy-start | bytes 25165828 | tf_op jit(solution)/shard_map/while
  75.1 5.8 %copy-start.1 = (f32[1024,2048]{1,0:T(8,128)S(1)}, f32[1024,2048]{1,0:T(8,128)}, u32[]{:S(2)}) copy-start(f32[1024,2048]{1,0:T(8,128)} %get-tuple-element.151) | copy-start | bytes 25165828 | tf_op jit(solution)/shard_map/while
  89.3 5.8 %copy-start.1 = (f32[1024,2048]{1,0:T(8,128)S(1)}, f32[1024,2048]{1,0:T(8,128)}, u32[]{:S(2)}) copy-start(f32[1024,2048]{1,0:T(8,128)} %get-tuple-element.151) | copy-start | bytes 25165828 | tf_op jit(solution)/shard_map/while
  103.4 5.8 %copy-start.1 = (f32[1024,2048]{1,0:T(8,128)S(1)}, f32[1024,2048]{1,0:T(8,128)}, u32[]{:S(2)}) copy-start(f32[1024,2048]{1,0:T(8,128)} %get-tuple-element.151) | copy-start | bytes 25165828 | tf_op jit(solution)/shard_map/while
  112.1 127.9 %copy-start.4 = (bf16[4,2,1,128]{3,1,2,0:T(2,128)(2,1)S(1)}, bf16[4,2,1,128]{3,1,2,0:T(2,128)(2,1)}, u32[]{:S(2)}) copy-start(bf16[4,2,1,128]{3,1,2,0:T(2,128)(2,1)} %param.17) | copy-start | bytes 6148
  244.8 307.6 %reduce-scatter.2.cloned.1.call-start = ((), (), s32[]{:S(2)}) async-start(), calls=%async_computation.2 | async-start | bytes 294912 | tf_op jit(solution)/shard_map/reduce_scatter | solution.py:170
Sparse Core Ops, SparseCore 0:
  244.9 271.5 all-reduce.1
  519.4 32.9 reduce-scatter.1
where the time goes:
time: 566 us; the launch traced here: 561 us
  blocking collectives  300 us (53%)
  waiting for transfers between devices  176 us (31%)
  matrix products  41.3 us (7%)
  other arithmetic  24.3 us (4%)
  between operations  13.5 us (2%)
    psum x1, waiting for transfers between devices, shards(): lax.psum((numerator * rescale[..., None], totals * rescale), 'seq')  143 us
    psum x1, blocking collectives, shards(): lax.psum((numerator * rescale[..., None], totals * rescale), 'seq')  129 us
    pmax x1, blocking collectives, shards(): global_max = lax.pmax(maximum, 'seq')  123 us
    all_gather x1, blocking collectives, shards(): gathered = absorb(lax.all_gather(queries, 'seq', axis=0, tiled=True))  47.9 us
    reduce_scatter x1, waiting for transfers between devices, shards(): lax.psum_scatter(jnp.einsum('rtk,kc->rtc', attended, out_weight, preferre...  33.1 us
    dot_general x4, matrix products, advance(): jnp.einsum('nd,kd->nk', query_rows, key_block, preferred_element_type=jnp...  21.7 us
    reduce_sum x4, other arithmetic, advance(): totals = totals * rescale + jnp.sum(weights, axis=1)  19.7 us
    dot_general x4, matrix products, advance(): jnp.dot(weights.astype(jnp.bfloat16), value_block, preferred_element_type...  11.7 us
  transfers between devices with their start and end apart: 2, of which 2 were waited for; matrix products, arithmetic and copies ran while one was open for 0% of the time, Pallas kernels for 0%

commit v1 on v0

v1 whole, which is shorter than its diff:
```python
import functools

import jax
import jax.numpy as jnp
from jax import lax
from jax.experimental import pallas as pl
from jax.experimental.pallas import tpu as pltpu
from jax.sharding import PartitionSpec as P

LOW = -1.0e30
LOG2E = 1.4426950408889634
STAT_ROWS = 16


def dot_rows(left, right):
    return lax.dot_general(
        left, right, (((1,), (1,)), ((), ())), preferred_element_type=jnp.float32
    )


def split_bf16(value):
    high = value.astype(jnp.bfloat16)
    rest = value - high.astype(jnp.float32)
    middle = rest.astype(jnp.bfloat16)
    low = (rest - middle.astype(jnp.float32)).astype(jnp.bfloat16)
    return high, middle, low


def prefix_kernel(query_ref, key_ref, value_ref, out_ref, *, key_block, group, scale):
    query_rows = query_ref[...]
    count, head_dim = query_rows.shape
    positions = key_ref.shape[0]
    top = jnp.full((count, 1), LOW, jnp.float32)
    total = jnp.zeros((count, head_dim), jnp.float32)
    acc = jnp.zeros((count, head_dim), jnp.float32)
    for start in range(0, positions, key_block):
        scores = dot_rows(query_rows, key_ref[start : start + key_block, :]) * scale
        new_top = jnp.maximum(top, jnp.max(scores, axis=1, keepdims=True))
        weights = jnp.exp2(scores - new_top)
        rescale = jnp.exp2(top - new_top)
        part = weights[:, :head_dim]
        for lane in range(head_dim, key_block, head_dim):
            part = part + weights[:, lane : lane + head_dim]
        total = total * rescale + part
        acc = acc * rescale + jnp.dot(
            weights.astype(jnp.bfloat16),
            value_ref[start : start + key_block, :],
            preferred_element_type=jnp.float32,
        )
        top = new_top
    total = jnp.sum(total, axis=1, keepdims=True)
    mean = (acc / total).astype(jnp.bfloat16)
    row = lax.broadcasted_iota(jnp.int32, (group, head_dim), 0)
    lane = lax.broadcasted_iota(jnp.int32, (group, head_dim), 1)
    for index in range(count // group):
        rows = slice(index * group, (index + 1) * group)
        stat = jnp.where(lane == row, top[rows], 0.0) + jnp.where(
            lane == row + group, total[rows], 0.0
        )
        stat = jnp.sum(stat, axis=0, keepdims=True)
        high, middle, low = split_bf16(stat)
        out_ref[index, :group, :] = mean[rows]
        tile_row = lax.broadcasted_iota(jnp.int32, (STAT_ROWS, head_dim), 0)
        tile = jnp.where(tile_row == 0, high.astype(jnp.float32), 0.0)
        tile = tile + jnp.where(tile_row == 1, middle.astype(jnp.float32), 0.0)
        tile = tile + jnp.where(tile_row == 2, low.astype(jnp.float32), 0.0)
        out_ref[index, group:, :] = tile.astype(jnp.bfloat16)


def prefix_parts(query_rows, key_rows, value_rows, group, scale):
    count, head_dim = query_rows.shape
    row_block = min(512, count)
    owners = row_block // group
    return pl.pallas_call(
        functools.partial(
            prefix_kernel, key_block=min(512, key_rows.shape[0]), group=group, scale=scale
        ),
        grid=(count // row_block,),
        in_specs=[
            pl.BlockSpec((row_block, head_dim), lambda i: (i, 0)),
            pl.BlockSpec(key_rows.shape, lambda i: (0, 0)),
            pl.BlockSpec(value_rows.shape, lambda i: (0, 0)),
        ],
        out_specs=pl.BlockSpec((owners, group + STAT_ROWS, head_dim), lambda i: (i, 0, 0)),
        out_shape=jax.ShapeDtypeStruct(
            (count // group, group + STAT_ROWS, head_dim), jnp.bfloat16
        ),
        compiler_params=pltpu.CompilerParams(vmem_limit_bytes=40 * 2**20),
        name="prefix_parts",
    )(query_rows, key_rows, value_rows)


def suffix_kernel(
    length_ref, query_ref, key_ref, value_ref, new_key_ref, new_value_ref,
    mean_ref, top_ref, total_ref, acc_ref, *, key_block, group_size, scale,
):
    request = pl.program_id(0)
    block = pl.program_id(1)
    length = length_ref[request]
    query_rows = query_ref[0]
    rows, head_dim = query_rows.shape

    @pl.when(block == 0)
    def _():
        new_keys = new_key_ref[0]
        count = new_keys.shape[0]
        scores = dot_rows(query_rows, new_keys) * scale
        step = lax.broadcasted_iota(jnp.int32, (rows, count), 0) // group_size
        slot = lax.broadcasted_iota(jnp.int32, (rows, count), 1)
        allowed = step >= slot
        scores = jnp.where(allowed, scores, LOW)
        top = jnp.max(scores, axis=1, keepdims=True)
        weights = jnp.where(allowed, jnp.exp2(scores - top), 0.0)
        rounded = weights.astype(jnp.bfloat16).astype(jnp.float32)
        values = new_value_ref[0].astype(jnp.float32)
        acc = rounded[:, 0:1] * values[0:1]
        for slot_index in range(1, count):
            acc = acc + rounded[:, slot_index : slot_index + 1] * values[slot_index : slot_index + 1]
        acc_ref[...] = acc
        top_ref[0] = jnp.broadcast_to(top, (rows, head_dim))
        total_ref[0] = jnp.broadcast_to(jnp.sum(weights, axis=1, keepdims=True), (rows, head_dim))

    @pl.when(block * key_block < length)
    def _():
        top = top_ref[0][:, 0:1]
        scores = dot_rows(query_rows, key_ref[0]) * scale
        slot = block * key_block + lax.broadcasted_iota(jnp.int32, scores.shape, 1)
        scores = jnp.where(slot < length, scores, LOW)
        new_top = jnp.maximum(top, jnp.max(scores, axis=1, keepdims=True))
        weights = jnp.exp2(scores - new_top)
        rescale = jnp.exp2(top - new_top)
        total_ref[0] = total_ref[0] * rescale + jnp.sum(weights, axis=1, keepdims=True)
        acc_ref[...] = acc_ref[...] * rescale + jnp.dot(
            weights.astype(jnp.bfloat16), value_ref[0], preferred_element_type=jnp.float32
        )
        top_ref[0] = jnp.broadcast_to(new_top, (rows, head_dim))

    @pl.when(block == pl.num_programs(1) - 1)
    def _():
        mean_ref[0] = acc_ref[...] / total_ref[0]


def suffix_part(query_rows, keys, values, new_keys, new_values, lengths, group_size, scale):
    requests, rows, head_dim = query_rows.shape
    slots = keys.shape[1]
    count = new_keys.shape[1]
    key_block = min(2048, slots)

    def held(r, b, length_ref):
        return (r, jnp.minimum(b, (length_ref[r] - 1) // key_block), 0)

    own = lambda r, b, length_ref: (r, 0, 0)
    shape = jax.ShapeDtypeStruct((requests, rows, head_dim), jnp.float32)
    return pl.pallas_call(
        functools.partial(suffix_kernel, key_block=key_block, group_size=group_size, scale=scale),
        grid_spec=pltpu.PrefetchScalarGridSpec(
            num_scalar_prefetch=1,
            grid=(requests, slots // key_block),
            in_specs=[
                pl.BlockSpec((1, rows, head_dim), own),
                pl.BlockSpec((1, key_block, head_dim), held),
                pl.BlockSpec((1, key_block, head_dim), held),
                pl.BlockSpec((1, count, head_dim), own),
                pl.BlockSpec((1, count, head_dim), own),
            ],
            out_specs=[pl.BlockSpec((1, rows, head_dim), own)] * 3,
            scratch_shapes=[pltpu.VMEM((rows, head_dim), jnp.float32)],
        ),
        out_shape=[shape] * 3,
        compiler_params=pltpu.CompilerParams(vmem_limit_bytes=24 * 2**20),
        name="suffix_part",
    )(lengths, query_rows, keys, values, new_keys, new_values)


def combine_kernel(part_ref, mean_ref, top_ref, total_ref, out_ref):
    senders, height, head_dim = part_ref.shape
    rows = height - STAT_ROWS
    stat = jnp.sum(part_ref[:, rows : rows + STAT_ROWS, :].astype(jnp.float32), axis=1)
    stat = stat.T
    own_top = top_ref[...][:, 0:1]
    own_total = total_ref[...][:, 0:1]
    tops, totals = stat[:rows], stat[rows : 2 * rows]
    peak = jnp.maximum(jnp.max(tops, axis=1, keepdims=True), own_top)
    weights = jnp.exp2(tops - peak) * totals
    own = jnp.exp2(own_top - peak) * own_total
    total = jnp.sum(weights, axis=1, keepdims=True) + own
    acc = mean_ref[...] * own
    for sender in range(senders):
        acc = acc + part_ref[sender, :rows, :].astype(jnp.float32) * weights[:, sender : sender + 1]
    out_ref[...] = (acc / total).astype(jnp.bfloat16)


def combine(parts, mean, top, total):
    rows, head_dim = mean.shape
    return pl.pallas_call(
        combine_kernel,
        out_shape=jax.ShapeDtypeStruct((rows, head_dim), jnp.bfloat16),
        name="combine_parts",
    )(parts, mean, top, total)


def shards(
    queries, prefix_keys, prefix_values, suffix_keys, suffix_values, new_keys, new_values,
    suffix_lengths, out_weight,
):
    owned, steps, row_width = queries.shape
    head_dim = prefix_keys.shape[2]
    group_size = row_width // head_dim
    group = owned * steps * group_size
    scale = head_dim**-0.5 * LOG2E
    everyone = owned * lax.axis_size("seq")
    own_rows = queries.reshape(group, head_dim)
    gathered = lax.all_gather(own_rows, "seq", axis=0, tiled=True)
    mean, top, total = suffix_part(
        own_rows.reshape(owned, steps * group_size, head_dim),
        suffix_keys[:, :, 0, :], suffix_values[:, :, 0, :],
        new_keys[:, :, 0, :], new_values[:, :, 0, :], suffix_lengths, group_size, scale,
    )
    parts = prefix_parts(gathered, prefix_keys[:, 0, :], prefix_values[:, 0, :], group, scale)
    parts = lax.all_to_all(parts, "seq", 0, 0, tiled=True)
    attended = combine(
        parts, mean.reshape(group, head_dim), top.reshape(group, head_dim),
        total.reshape(group, head_dim),
    )
    attended = attended.reshape(owned * steps, row_width)
    attended = lax.all_gather(attended, "seq", axis=0, tiled=True)
    partial = jnp.dot(attended, out_weight, preferred_element_type=jnp.float32)
    columns = out_weight.shape[1]
    heads = lax.axis_size("head")
    partial = partial.astype(jnp.bfloat16).reshape(heads, everyone * steps // heads, columns)
    partial = lax.all_to_all(partial, "head", 0, 0, tiled=True)
    summed = jnp.sum(partial.astype(jnp.float32), axis=0).astype(jnp.bfloat16)
    return summed.reshape(everyone // heads, steps, columns)


def solution(mesh):
    placed = (
        P("seq", None, "head"),
        P("seq", "head", None),
        P("seq", "head", None),
        P("seq", None, "head", None),
        P("seq", None, "head", None),
        P("seq", None, "head", None),
        P("seq", None, "head", None),
        P("seq"),
        P("head", "seq"),
    )
    return jax.shard_map(
        shards, mesh=mesh, in_specs=placed, out_specs=P("head", None, "seq"), check_vma=False
    )
```

time: 566 us -> 146 us (0.26)
  blocking collectives: 300 us -> 99.2 us
  waiting for transfers between devices: 176 us -> 9.52 us
  matrix products: 41.3 us -> 0.3 us
  other arithmetic: 24.3 us -> 0.02 us
  Pallas kernels: 0 us -> 21.3 us
  between operations: 13.5 us -> 0.11 us
  local copies, waits for them, and re-layouts: 5.5 us -> 11.6 us
    psum x1 -> x0, waiting for transfers between devices: 143 us -> none  [shards(): lax.psum((numerator * rescale[..., None], totals * rescale), 'seq')]
    psum x1 -> x0, blocking collectives: 129 us -> none  [shards(): lax.psum((numerator * rescale[..., None], totals * rescale), 'seq')]
    pmax x1 -> x0, blocking collectives: 123 us -> none  [shards(): global_max = lax.pmax(maximum, 'seq')]
    all_gather x1 -> x2, blocking collectives: 47.9 us -> 89.2 us  [the longest x1 47.5 us: shards(): gathered = lax.all_gather(own_rows, 'seq', axis=0, tiled=True)]
    dot_general x13 -> x1, matrix products: 41.3 us -> 0.3 us  [shards(): partial = jnp.dot(attended, out_weight, preferred_element_type=jnp.float32)]
    reduce_scatter x1 -> x0, waiting for transfers between devices: 33.1 us -> none  [shards(): lax.psum_scatter(jnp.einsum('rtk,kc->rtc', attended, out_weight, preferre...]
    pallas_call x0 -> x3, Pallas kernels: none -> 21.3 us  [the longest x1 14.6 us: prefix_parts(): pl.pallas_call(functools.partial(prefix_kernel, key_block=min(512, key_ro...]
    reduce_sum x6 -> x1, other arithmetic: 20.2 us -> 0.02 us  [shards(): summed = jnp.sum(partial.astype(jnp.float32), axis=0).astype(jnp.bfloat16)]
  transfers between devices with their start and end apart: 2 -> 1, of which waited for: 2 -> 1; matrix products, arithmetic and copies ran while one was open for 0% -> 0% of each run, Pallas kernels for 0% -> 3%
where the time goes in v1:
time: 146 us
  blocking collectives  99.2 us (68%)
  Pallas kernels  21.3 us (15%)
  local copies, waits for them, and re-layouts  11.6 us (8%)
  waiting for transfers between devices  9.52 us (7%)
  starting transfers between devices  3.72 us (3%)
    all_gather x1, blocking collectives, shards(): gathered = lax.all_gather(own_rows, 'seq', axis=0, tiled=True)  47.5 us
    all_gather x1, blocking collectives, shards(): attended = lax.all_gather(attended, 'seq', axis=0, tiled=True)  41.7 us
    pallas_call x1, Pallas kernels, prefix_parts(): pl.pallas_call(functools.partial(prefix_kernel, key_block=min(512, key_ro...  14.6 us
    all_to_all x1, blocking collectives, shards(): partial = lax.all_to_all(partial, 'head', 0, 0, tiled=True)  10.1 us
    all_to_all x1, waiting for transfers between devices, shards(): parts = lax.all_to_all(parts, 'seq', 0, 0, tiled=True)  9.52 us
    unnamed x26, local copies, waits for them, and re-layouts  9.49 us
    pallas_call x1, Pallas kernels, suffix_part(): pl.pallas_call(functools.partial(suffix_kernel, key_block=key_block, grou...  4.27 us
    all_to_all x1, starting transfers between devices, shards(): parts = lax.all_to_all(parts, 'seq', 0, 0, tiled=True)  3.72 us
  transfers between devices with their start and end apart: 1, of which 1 were waited for; matrix products, arithmetic and copies ran while one was open for 0% of the time, Pallas kernels for 3%

profile of v1, /device:TPU:1, one launch (start us, length us, event | category | flops | bytes accessed | tf_op | source)
XLA Modules:
  0.0 145.9 jit_solution(7771941870867201453)
XLA Ops:
  0.0 0.0 copy-start
  0.0 0.0 copy-start.12
  0.0 0.0 copy-start.10
  0.0 0.0 copy-start.8
  0.0 0.0 copy-start.9
  0.0 0.8 reshape.21
  0.8 47.5 %all_gather.6.query_ref = bf16[2048,128]{1,0:T(8,128)(2,1)S(1)} all-gather(bf16[64,128]{1,0:T(8,128)(2,1)S(1)} %reshape.21), channel_id=1, replica_groups=mesh['seq'=32,'head'=8] {'seq'}, dimensions={0}, use_global_device_ids=true | all-gather | bytes 540672 | tf_op jit(solution)/shard_map/all_gather | solution.py:213
  48.3 1.2 copy-done.3
  49.5 1.2 copy-done.4
  50.7 14.6 %prefix_parts.1 = bf16[32,80,128]{2,1,0:T(8,128)(2,1)} custom-call(bf16[2048,128]{1,0:T(8,128)(2,1)S(1)} %all_gather.6.query_ref, bf16[4096,128]{1,0:T(8,128)(2,1)S(1)} %bitcast.14, bf16[4096,128]{1,0:T(8,128)(2,1)S(1)} %bitcast.15), custom_call_target="tpu_custom_call" | custom-call | tf_op jit(solution)/shard_map/prefix_parts/pallas_call | solution.py:74
  65.3 3.7 %all-to-all-start = ((bf16[32,80,128]{2,1,0:T(8,128)(2,1)}), bf16[32,80,128]{2,1,0:T(8,128)(2,1)S(1)}, u32[]{:S(2)}, u32[]{:S(2)}) async-start(bf16[32,80,128]{2,1,0:T(8,128)(2,1)} %prefix_parts.1), calls=%async_computation | async-start | bytes 1310720 | tf_op jit(solution)/shard_map/all_to_all | solution.py:220
  69.0 0.0 copy-done.12
  69.1 0.0 copy-done.10
  69.1 0.0 copy-done.8
  69.1 0.0 copy-done.9
  69.1 0.0 copy-start.1
  69.1 2.2 %copy-done.1 = bf16[4,4096,1,128]{3,1,2,0:T(8,128)(2,1)S(1)} copy-done((bf16[4,4096,1,128]{3,1,2,0:T(8,128)(2,1)S(1)}, bf16[4,4096,1,128]{3,1,2,0:T(8,128)(2,1)}, u32[]{:S(2)}) %copy-start.1) | copy-done | bytes 4194328
  71.3 2.2 %copy-done.2 = bf16[4,4096,1,128]{3,1,2,0:T(8,128)(2,1)S(1)} copy-done((bf16[4,4096,1,128]{3,1,2,0:T(8,128)(2,1)S(1)}, bf16[4,4096,1,128]{3,1,2,0:T(8,128)(2,1)}, u32[]{:S(2)}) %copy-start.2) | copy-done | bytes 4194328
  73.5 4.3 %suffix_part.1 = (f32[4,16,128]{2,1,0:T(8,128)S(1)}, f32[4,16,128]{2,1,0:T(8,128)S(1)}, f32[4,16,128]{2,1,0:T(8,128)S(1)}) custom-call(s32[4]{0:T(128)S(1)} %copy-done.10, bf16[4,16,128]{2,1,0:T(8,128)(2,1)S(1)} %reshape_reshape.3.query_ref, bf16[4,4096,128]{2,1,0:T(8,128)(2,1)S(1)} %bitcast.12, bf16[4,4096,128]{2,1,0:T(8,128)(2,1)S(1)} %bitcast.13, ...), custom_call_target="tpu_custom_call" | custom-call | tf_op jit(solution)/shard_map/suffix_part/pallas_call | solution.py:154
  77.8 0.0 copy-start.5
  77.8 0.6 copy-done.5
  78.4 0.6 copy-done.6
  79.0 0.6 copy-done.7
  79.6 9.5 %all-to-all-done.part_ref = bf16[32,80,128]{2,1,0:T(8,128)(2,1)S(1)} async-done(((bf16[32,80,128]{2,1,0:T(8,128)(2,1)}), bf16[32,80,128]{2,1,0:T(8,128)(2,1)S(1)}, u32[]{:S(2)}, u32[]{:S(2)}) %all-to-all-start) | async-done | bytes 655392 | tf_op jit(solution)/shard_map/all_to_all | solution.py:220
  89.1 0.8 copy-done.11
  89.9 2.5 %combine_parts.1 = bf16[64,128]{1,0:T(8,128)(2,1)} custom-call(bf16[32,80,128]{2,1,0:T(8,128)(2,1)} %copy-done.11, f32[64,128]{1,0:T(8,128)} %bitcast.16, f32[64,128]{1,0:T(8,128)} %bitcast.17, f32[64,128]{1,0:T(8,128)} %bitcast.18), custom_call_target="tpu_custom_call" | custom-call | tf_op jit(solution)/shard_map/combine_parts/pallas_call | solution.py:195
  92.4 0.7 reshape.25
  93.2 41.7 %all_gather.7 = bf16[256,1024]{1,0:T(8,128)(2,1)S(1)} all-gather(bf16[8,1024]{1,0:T(8,128)(2,1)S(1)} %reshape.25), channel_id=1, replica_groups=mesh['seq'=32,'head'=8] {'seq'}, dimensions={0}, use_global_device_ids=true | all-gather | bytes 540672 | tf_op jit(solution)/shard_map/all_gather | solution.py:226
  134.9 0.0 copy-done
  134.9 0.3 convolution_convert_fusion
  135.2 10.1 %all_to_all.10 = bf16[8,32,256]{2,1,0:T(8,128)(2,1)S(1)} all-to-all(bf16[8,32,256]{2,1,0:T(8,128)(2,1)S(1)} %bitcast.21), channel_id=1, replica_groups=mesh['seq'=32,'head'=8] {'head'}, dimensions={0} | all-to-all | bytes 262144 | tf_op jit(solution)/shard_map/all_to_all | solution.py:231
  145.3 0.6 reshape.27
  (8 shorter events, 0.1 us)
Async XLA Ops:
  0.0 134.9 %copy-start = (bf16[1024,256]{1,0:T(8,128)(2,1)S(1)}, bf16[1024,256]{1,0:T(8,128)(2,1)}, u32[]{:S(2)}) copy-start(bf16[1024,256]{1,0:T(8,128)(2,1)} %param.17) | copy-start | bytes 1572868
  0.0 69.0 %copy-start.12 = (bf16[4,2,1024]{2,1,0:T(2,128)(2,1)S(1)}, bf16[4,2,1024]{2,1,0:T(2,128)(2,1)}, u32[]{:S(2)}) copy-start(bf16[4,2,1024]{2,1,0:T(2,128)(2,1)} %param.9) | copy-start | bytes 49156
  0.0 69.1 %copy-start.10 = (s32[4]{0:T(128)S(1)}, s32[4]{0:T(128)}, u32[]{:S(2)}) copy-start(s32[4]{0:T(128)} %length_ref.1) | copy-start | bytes 52
  0.0 69.1 %copy-start.8 = (bf16[4,2,1,128]{3,1,2,0:T(2,128)(2,1)S(1)}, bf16[4,2,1,128]{3,1,2,0:T(2,128)(2,1)}, u32[]{:S(2)}) copy-start(bf16[4,2,1,128]{3,1,2,0:T(2,128)(2,1)} %param.14) | copy-start | bytes 6148
  0.0 69.1 %copy-start.9 = (bf16[4,2,1,128]{3,1,2,0:T(2,128)(2,1)S(1)}, bf16[4,2,1,128]{3,1,2,0:T(2,128)(2,1)}, u32[]{:S(2)}) copy-start(bf16[4,2,1,128]{3,1,2,0:T(2,128)(2,1)} %param.15) | copy-start | bytes 6148
  48.3 1.2 copy-start.3
  49.5 1.2 copy-start.4
  65.3 23.8 %all-to-all-start = ((bf16[32,80,128]{2,1,0:T(8,128)(2,1)}), bf16[32,80,128]{2,1,0:T(8,128)(2,1)S(1)}, u32[]{:S(2)}, u32[]{:S(2)}) async-start(bf16[32,80,128]{2,1,0:T(8,128)(2,1)} %prefix_parts.1), calls=%async_computation | async-start | bytes 1310720 | tf_op jit(solution)/shard_map/all_to_all | solution.py:220
  69.1 2.2 %copy-start.1 = (bf16[4,4096,1,128]{3,1,2,0:T(8,128)(2,1)S(1)}, bf16[4,4096,1,128]{3,1,2,0:T(8,128)(2,1)}, u32[]{:S(2)}) copy-start(bf16[4,4096,1,128]{3,1,2,0:T(8,128)(2,1)} %param.12) | copy-start | bytes 12582916
  71.3 2.2 %copy-start.2 = (bf16[4,4096,1,128]{3,1,2,0:T(8,128)(2,1)S(1)}, bf16[4,4096,1,128]{3,1,2,0:T(8,128)(2,1)}, u32[]{:S(2)}) copy-start(bf16[4,4096,1,128]{3,1,2,0:T(8,128)(2,1)} %param.13) | copy-start | bytes 12582916
  77.8 0.6 copy-start.5
  78.4 0.6 copy-start.6
  79.0 0.6 copy-start.7
  89.1 0.9 copy-start.11
